TPU v7x, 256 devices: a whole 4x4x8 slice. The times are simulated.
256 devices in a mesh: tm: 32 (over z, y), freq: 8 (over x, core).
Axes of the slice: x: 4, y: 4, z: 8, core: 2. Of those that a mesh axis runs over, the one named last changes fastest.
Arguments:
- snapshots: bfloat16 [4096, 32768], P('tm', 'freq'), may hold values from -8 to 8
Outputs:
- basis: bfloat16 [120, 62, 32768], P('freq', None, 'tm')
- factor: float32 [120, 62, 62], P('freq')
All inputs are finite; a program needn't handle non-finite values.
Results may differ from a plain program's by a relative error of at most 0.0065.
Values may be sent and summed in bfloat16 or wider, within the bound.
A program may use at most 128 MiB of HBM per device.

v0:
```python
import math

import jax
import jax.numpy as jnp
from jax import lax
from jax.sharding import PartitionSpec as P

K = 120


def passed_along(value, axis, by):
    devices = lax.axis_size(axis)
    pairs = [(i, i + by) for i in range(devices) if 0 <= i + by < devices]
    return lax.ppermute(value, axis, pairs)


def fourier_table(num_bins, half_len, which_half):
    bins_col = jnp.arange(1, num_bins + 1, dtype=jnp.int32)[:, None]
    sample = jnp.arange(half_len, dtype=jnp.int32)[None, :] + which_half * half_len
    length = 2 * half_len
    phase_idx = (bins_col * sample % length).astype(jnp.float32) * (2.0 * math.pi / length)
    window = 0.5 - 0.5 * jnp.cos(sample.astype(jnp.float32) * (2.0 * math.pi / length))
    stacked = jnp.stack([window * jnp.cos(phase_idx), -window * jnp.sin(phase_idx)], axis=1)
    return stacked.reshape(2 * num_bins, half_len).astype(jnp.bfloat16)


def on_device(snapshots):
    high = lax.Precision.HIGHEST
    half_len = snapshots.shape[0]
    local_rows = snapshots.shape[1]
    own_table = fourier_table(K, half_len, 0)
    next_table = fourier_table(K, half_len, 1)
    own_term = jnp.dot(own_table, snapshots, preferred_element_type=jnp.float32)
    next_term = jnp.dot(next_table, snapshots, preferred_element_type=jnp.float32).astype(
        jnp.bfloat16
    )
    next_term = passed_along(next_term, "tm", -1)
    spectra = (own_term + next_term.astype(jnp.float32)).astype(jnp.bfloat16)
    shaped = spectra.reshape(K, 2, 1, local_rows)
    arrived = lax.all_to_all(
        lax.all_to_all(shaped, "freq", split_axis=0, concat_axis=3, tiled=True),
        "tm",
        split_axis=3,
        concat_axis=2,
        tiled=True,
    )
    tm_size = lax.axis_size("tm")
    groups = arrived.shape[0]
    row_count = arrived.shape[3]
    width = 2 * (tm_size - 1)
    columns = arrived[:, :, : tm_size - 1, :].reshape(groups, width, row_count)
    total_rows = row_count * tm_size
    local_gram = jnp.einsum("fcr,fdr->fcd", columns, columns, preferred_element_type=jnp.float32)
    gram_matrix = lax.psum(local_gram, "tm") / total_rows
    lower_factor = jnp.linalg.cholesky(gram_matrix)
    identity = jnp.broadcast_to(jnp.eye(width, dtype=jnp.float32), gram_matrix.shape)
    inverse_lower = jax.scipy.linalg.solve_triangular(lower_factor, identity, lower=True)
    basis_full = jnp.einsum(
        "fcd,fdr->fcr", inverse_lower, columns.astype(jnp.float32), precision=high
    )
    return (basis_full.astype(jnp.bfloat16), jnp.transpose(lower_factor, (0, 2, 1)))


def solution(mesh):
    placed = (P("tm", "freq"),)
    return jax.shard_map(
        on_device,
        mesh=mesh,
        in_specs=placed,
        out_specs=(P("freq", None, "tm"), P("freq", None, None)),
        check_vma=False,
    )
```

profile of v0, /device:TPU:16, one launch (start us, length us, event | category | flops | bytes accessed | tf_op | source)
XLA Modules:
  0.0 599.6 jit_solution(6969312997901257062)
XLA Ops:
  7.4 0.6 multiply_convert_fusion.1
  8.1 0.3 copy-done
  8.4 0.7 convolution_convert_fusion
  9.1 2.4 collective-permute-start
  11.5 44.0 %collective-permute-done = bf16[240,4096]{1,0:T(8,128)(2,1)S(1)} collective-permute-done((bf16[240,4096]{1,0:T(8,128)(2,1)S(1)}, bf16[240,4096]{1,0:T(8,128)(2,1)S(1)}, u32[]{:S(2)}, u32[]{:S(2)}) %collective-permute-start) | collective-permute-done | bytes 1966112 | tf_op jit(solution)/shard_map/ppermute | solution.py:14
  55.5 0.7 add_convert_fusion
  56.2 2.5 reshape.364
  58.7 30.4 %all_to_all.30 = bf16[120,2,1,4096]{3,1,2,0:T(2,128)(2,1)S(1)} all-to-all(bf16[120,2,1,4096]{3,1,2,0:T(2,128)(2,1)} %bitcast.31), channel_id=1, replica_groups=mesh['tm'=32,'freq'=8] {'freq'}, dimensions={0} | all-to-all | bytes 3932160 | tf_op jit(solution)/shard_map/all_to_all | solution.py:41
  89.1 27.6 %copy.58 = bf16[15,2,1,8,4096]{0,1,4,3,2:T(2,128)(2,1)} copy(bf16[15,2,1,8,4096]{4,1,0,3,2:T(2,128)(2,1)S(1)} %bitcast.32) | data formatting | bytes 3932160 | tf_op jit(solution)/shard_map/all_to_all | solution.py:41
  116.7 26.3 %reshape.366 = bf16[32,2,15360]{2,1,0:T(2,128)(2,1)S(1)} reshape(bf16[32768,1,2,15]{3,2,1,0:T(2,128)(2,1)} %bitcast.29) | data formatting | bytes 3932160
  143.0 61.0 %all_to_all.31 = bf16[32,2,15360]{2,1,0:T(2,128)(2,1)} all-to-all(bf16[32,2,15360]{2,1,0:T(2,128)(2,1)S(1)} %reshape.366), channel_id=1, replica_groups=mesh['tm'=32,'freq'=8] {'tm'}, dimensions={0} | all-to-all | bytes 3932160 | tf_op jit(solution)/shard_map/all_to_all | solution.py:40
  203.9 40.5 %reshape.367 = bf16[32768,1,2,15]{3,2,1,0:T(2,128)(2,1)} reshape(bf16[32,2,15360]{2,1,0:T(2,128)(2,1)} %all_to_all.31) | data formatting | bytes 3932160
  244.4 13.7 %slice.16 = bf16[15,2,31,1024]{0,1,3,2:T(2,128)(2,1)} slice(bf16[15,2,32,1024]{0,1,3,2:T(2,128)(2,1)} %bitcast.30), slice={[0:15], [0:2], [0:31], [0:1024]} | slice | bytes 3809280 | tf_op jit(solution)/shard_map/slice | solution.py:51
  258.1 24.7 %copy.60 = bf16[15,2,31,1024]{3,2,1,0:T(8,128)(2,1)} copy(bf16[15,2,31,1024]{0,1,3,2:T(2,128)(2,1)} %slice.16) | data formatting | bytes 3809280
  282.8 2.4 reshape.365
  285.2 1.4 fusion.17
  286.8 140.8 %all-reduce.2.cloned.1.call-done = f32[15,62,62]{1,2,0:T(8,128)} async-done(((f32[15,62,62]{1,2,0:T(8,128)}), f32[15,62,62]{1,2,0:T(8,128)}) %all-reduce.2.cloned.1.call-update) | async-done | bytes 230656 | tf_op jit(solution)/shard_map/psum | solution.py:54
  427.6 1.1 broadcast_multiply_fusion
  428.7 0.3 copy.53
  429.0 85.2 %custom-call.8 = f32[15,62,62]{2,1,0:T(8,128)S(1)} custom-call(f32[15,62,62]{2,1,0:T(8,128)S(1)} %fusion.2), custom_call_target="Cholesky" | custom-call | tf_op jit(solution)/shard_map/jit(cholesky)/cholesky | solution.py:55
  514.6 72.1 %custom-call.9 = f32[15,1,62,62]{2,3,1,0:T(8,128)} custom-call(f32[15,1,62,62]{3,2,1,0:T(8,128)S(1)} %get-tuple-element.19), custom_call_target="InvertDiagBlocksLowerTriangular" | custom-call | tf_op jit(solution)/shard_map/jit(_solve_triangular)/vmap()/triangular_solve | solution.py:57
  586.7 2.1 fusion
  588.7 3.0 convolution_convert_fusion.1
  591.7 1.0 copy.55
  (23 shorter events, 0.8 us)
Async XLA Ops:
  7.2 1.2 copy-start
  7.2 420.4 %all-reduce.2.cloned.1.call-start = ((), (), s32[]{:S(2)}) async-start(), calls=%async_computation.2 | async-start | bytes 983040 | tf_op jit(solution)/shard_map/psum | solution.py:54
  9.1 46.5 %collective-permute-start = (bf16[240,4096]{1,0:T(8,128)(2,1)S(1)}, bf16[240,4096]{1,0:T(8,128)(2,1)S(1)}, u32[]{:S(2)}, u32[]{:S(2)}) collective-permute-start(bf16[240,4096]{1,0:T(8,128)(2,1)S(1)} %convolution_convert_fusion), channel_id=1, source_target_pairs={{8,0},{16,8},{24,16},{32,24},{40,32},{48,40},{56,48},{64,56},{72,6... | collective-permute-start | bytes 5898248 | tf_op jit(solution)/shard_map/ppermute | solution.py:14
  427.5 1.4 copy-start.2
  586.7 6.1 %copy-start.1 = (bf16[128,4096]{1,0:T(8,128)(2,1)S(1)}, bf16[128,4096]{1,0:T(8,128)(2,1)}, u32[]{:S(2)}) copy-start(bf16[128,4096]{1,0:T(8,128)(2,1)} %param.1) | copy-start | bytes 3145732
Sparse Core Ops, SparseCore 0:
  286.8 140.6 all-reduce.1
where the time goes:
time: 602 us; the launch traced here: 600 us
  waiting for transfers between devices  185 us (31%)
  other arithmetic  160 us (27%)
  local copies, waits for them, and re-layouts  139 us (23%)
  blocking collectives  91.3 us (15%)
  between operations  14.2 us (2%)
  matrix products  7.79 us (1%)
    psum x1, waiting for transfers between devices, on_device(): gram_matrix = lax.psum(local_gram, 'tm') / total_rows  141 us
    unnamed x10, local copies, waits for them, and re-layouts  92.7 us
    another operation x4, other arithmetic, on_device(): lower_factor = jnp.linalg.cholesky(gram_matrix)  85.4 us
    another operation x2, other arithmetic, on_device(): jax.scipy.linalg.solve_triangular(lower_factor, identity, lower=True)  72.1 us
    all_to_all x1, blocking collectives, on_device(): lax.all_to_all(lax.all_to_all(shaped, 'freq', split_axis=0, concat_axis=3...  61 us
    ppermute x1, waiting for transfers between devices, passed_along(): return lax.ppermute(value, axis, pairs)  44 us
    all_to_all x1, blocking collectives, on_device(): lax.all_to_all(shaped, 'freq', split_axis=0, concat_axis=3, tiled=True)  30.4 us
    all_to_all x1, local copies, waits for them, and re-layouts, on_device(): lax.all_to_all(shaped, 'freq', split_axis=0, concat_axis=3, tiled=True)  27.6 us
  transfers between devices with their start and end apart: 2, of which 2 were waited for; matrix products, arithmetic and copies ran while one was open for 0% of the time, Pallas kernels for 0%

commit v1 on v0

v1 whole, which is shorter than its diff:
```python
import math

import jax
import jax.numpy as jnp
import numpy as np
from jax import lax
from jax.experimental import pallas as pl
from jax.experimental.pallas import tpu as pltpu
from jax.sharding import PartitionSpec as P

MESH = pl.DeviceIdType.MESH
K = 120
HALF = 128
TM = 32
FREQ = 8
BINS = K // FREQ
BLOCKS = TM - 1
COLS = 2 * BLOCKS
GROUP = 8
GROUPS = TM // GROUP
TILE = 2 * GROUP
PART = BINS * TILE
LANES = 128
SLABS = GROUP + 1
DEPTH = SLABS * HALF
SUB = 4
ROWS_HERE = FREQ * LANES
TOTAL_ROWS = TM * ROWS_HERE


def band_table():
    bins = np.arange(1, K + 1, dtype=np.int64)[:, None]
    sample = np.arange(2 * HALF, dtype=np.int64)[None, :]
    phase = (bins * sample % (2 * HALF)) * (2.0 * math.pi / (2 * HALF))
    window = 0.5 - 0.5 * np.cos(sample * (2.0 * math.pi / (2 * HALF)))
    table = np.stack([window * np.cos(phase), -window * np.sin(phase)], axis=1)
    table = table.astype(np.float32)
    band = np.zeros((K, 2, GROUP, SLABS * HALF), np.float32)
    for b in range(GROUP):
        band[:, :, b, b * HALF : (b + 2) * HALF] = table
    return band.reshape(K * TILE, DEPTH).astype(jnp.bfloat16)


def nt_dot(a, b):
    return lax.dot_general(a, b, (((1,), (1,)), ((), ())), preferred_element_type=jnp.float32)


def natural_rows(dst, value):
    for p in range(2):
        for g in range(GROUPS):
            r = TILE * g + GROUP * p
            dst[pl.ds(BLOCKS * p + GROUP * g, GROUP), :] = value[r : r + GROUP, :]


def eliminate(m):
    row = lax.broadcasted_iota(jnp.int32, (8, 128), 0)
    full = (8, 128)
    for j in range(0, COLS, 2):
        b, s = divmod(j, 8)
        r0 = jnp.broadcast_to(m[b][s : s + 1, :], full)
        r1 = jnp.broadcast_to(m[b][s + 1 : s + 2, :], full)
        a00 = jnp.broadcast_to(m[b][s : s + 1, j : j + 1], full)
        a01 = jnp.broadcast_to(m[b][s : s + 1, j + 1 : j + 2], full)
        a11 = jnp.broadcast_to(m[b][s + 1 : s + 2, j + 1 : j + 2], full)
        i0 = lax.rsqrt(a00)
        l10 = a01 * i0
        i1 = lax.rsqrt(a11 - l10 * l10)
        q0 = r0 * i0
        q1 = (r1 - l10 * q0) * i1
        for i in range(b, 8):
            c0 = jnp.broadcast_to(m[i][:, j : j + 1], full)
            c1 = jnp.broadcast_to(m[i][:, j + 1 : j + 2], full)
            m0 = c0 * i0
            m1 = (c1 - l10 * m0) * i1
            u = m[i] - m0 * q0 - m1 * q1
            if i == b:
                u = jnp.where(row > s + 1, u, m[i])
                u = jnp.where(row == s, q0, u)
                u = jnp.where(row == s + 1, q1, u)
            m[i] = u
    return m


def kernel(
    x_ref, band_hbm, basis_ref, factor_ref,
    band, mid, xt, spec, held, cols, gpart, grecv, res, perm,
    band_sem, l_sem, a_send, a_recv, b_send, b_recv, c_send, c_recv,
    g_send, g_recv, r_send, r_recv,
):
    t = lax.axis_index("tm")
    f = lax.axis_index("freq")
    z, y = t // SUB, t % SUB

    def colblock(j):
        return x_ref.at[:, pl.ds(pl.multiple_of(j * LANES, LANES), LANES)]

    def freq_peer(i):
        return lax.rem(f + i, FREQ)

    def tm_peer(i):
        return lax.rem(t + i, TM)

    def remote(src, dst, send, recv, to):
        return pltpu.make_async_remote_copy(
            src, dst, send, recv, device_id=to, device_id_type=MESH
        )

    def each(lo, hi, body):
        def step(i, carry):
            body(i)
            return carry

        lax.fori_loop(lo, hi, step, 0)

    load_band = pltpu.make_async_copy(band_hbm, band, band_sem)
    load_band.start()

    barrier = pltpu.get_barrier_semaphore()
    each(1, FREQ, lambda i: pl.semaphore_signal(
        barrier, inc=1, device_id=(t, freq_peer(i)), device_id_type=MESH))
    each(1, TM, lambda i: pl.semaphore_signal(
        barrier, inc=1, device_id=(tm_peer(i), f), device_id_type=MESH))
    pl.semaphore_wait(barrier, FREQ - 1 + TM - 1)

    def a_copy(i, s):
        to = freq_peer(i)
        return remote(colblock(FREQ * s + to), mid.at[SUB * f + s], a_send.at[i, s],
                      a_recv.at[f, s], (t, to))

    for s in range(SUB):
        each(1, FREQ, lambda i: a_copy(i, s).start())
        pltpu.make_async_copy(colblock(FREQ * s + f), mid.at[SUB * f + s], l_sem.at[s]).start()
    for s in range(SUB):
        pltpu.make_async_copy(colblock(FREQ * s + f), mid.at[SUB * f + s], l_sem.at[s]).wait()

    xt[TM] = jnp.zeros((HALF, LANES), jnp.bfloat16)

    def b_copy(n):
        return remote(mid.at[n], xt.at[t], b_send.at[n], b_recv.at[t], (n, f))

    def b_step(i):
        d = i // SUB
        dz = jnp.where(d % 2 == 1, (d + 1) // 2, FREQ - d // 2)
        ff = lax.rem(z + dz, FREQ)
        s = lax.rem(y + i, SUB)
        n = SUB * ff + s

        @pl.when(ff != f)
        def _():
            remote(mid.at[n], mid.at[n], a_send.at[0, 0], a_recv.at[ff, s], (t, f)).wait_recv()

        @pl.when(n != t)
        def _():
            b_copy(n).start()

        @pl.when(n == t)
        def _():
            pltpu.make_async_copy(mid.at[n], xt.at[t], l_sem.at[0]).start()

    each(0, TM, b_step)
    pltpu.make_async_copy(mid.at[t], xt.at[t], l_sem.at[0]).wait()
    load_band.wait()

    first = lax.rem(lax.rem(z + FREQ - 1, FREQ) // 2, GROUPS)

    def lanes_of(ff):
        return pl.ds(pl.multiple_of(ff * LANES, LANES), LANES)

    def piece(ff):
        return pl.ds(pl.multiple_of(ff * PART, PART), PART)

    def c_copy(i, g):
        to = freq_peer(i)
        return remote(spec.at[g, piece(to), :], held.at[g, :, lanes_of(f)],
                      c_send.at[i, g], c_recv.at[f, g], (t, to))

    def wait_slab(i):
        n = lax.rem(GROUP * first + i, TM)

        @pl.when(n != t)
        def _():
            remote(xt.at[n], xt.at[n], b_send.at[0], b_recv.at[n], (t, f)).wait_recv()

    def make_group(step, carry):
        g = lax.rem(first + step, GROUPS)
        lo = jnp.where(step == 0, 0, GROUP * step + 1)
        hi = jnp.minimum(GROUP * step + GROUP + 1, TM)
        each(lo, hi, wait_slab)
        stack = xt[pl.ds(GROUP * g, SLABS)].reshape(DEPTH, LANES)

        def part(i):
            to = freq_peer(i)
            rows = piece(to)
            value = jnp.dot(band[rows, :], stack, preferred_element_type=jnp.float32)
            spec[g, rows, :] = value.astype(jnp.bfloat16)

        def send_part(i):
            part(i)
            c_copy(i, g).start()

        each(1, FREQ, send_part)
        part(0)
        pltpu.make_async_copy(spec.at[g, piece(f), :], held.at[g, :, lanes_of(f)], l_sem.at[g]).start()
        return carry

    lax.fori_loop(0, GROUPS, make_group, 0)

    def wait_group(g):
        pltpu.make_async_copy(spec.at[g, piece(f), :], held.at[g, :, lanes_of(f)], l_sem.at[g]).wait()

        def wait_piece(i):
            ff = freq_peer(i)
            remote(spec.at[g, piece(ff), :], held.at[g, :, lanes_of(ff)],
                   c_send.at[0, 0], c_recv.at[ff, g], (t, f)).wait_recv()

        each(1, FREQ, wait_piece)

    each(0, GROUPS, wait_group)

    def owner(k):
        return 2 * k + f % 2

    def bin_columns(k):
        return jnp.concatenate(
            [held[g, pl.ds(pl.multiple_of(TILE * k, TILE), TILE), :] for g in range(GROUPS)], axis=0)

    def g_copy(k):
        return remote(gpart.at[k], grecv.at[t], g_send.at[k], g_recv.at[t], (owner(k), f))

    def gram(k):
        a = bin_columns(k)
        gm = nt_dot(a, a)
        gpart[k] = jnp.concatenate([gm[:32], gm[32:]], axis=1)

        @pl.when(owner(k) != t)
        def _():
            g_copy(k).start()

        @pl.when(owner(k) == t)
        def _():
            pltpu.make_async_copy(gpart.at[k], grecv.at[t], l_sem.at[0]).start()

    each(0, BINS, gram)

    r = lax.broadcasted_iota(jnp.int32, (64, 64), 0)
    c = lax.broadcasted_iota(jnp.int32, (64, 64), 1)
    block = GROUP * (c // TILE) + c % GROUP
    to_row = BLOCKS * (c % TILE // GROUP) + block
    order = jnp.where((r == to_row) & (block < BLOCKS), 1.0, 0.0).astype(jnp.bfloat16)

    def reorder(k):
        cols[k] = jnp.dot(order, bin_columns(k), preferred_element_type=jnp.float32).astype(
            jnp.bfloat16)

    each(0, BINS, reorder)

    mine = t // 2
    is_owner = (t % 2 == f % 2) & (mine < BINS)

    def r_copy(i):
        return remote(res.at[mine], res.at[mine], r_send.at[i], r_recv.at[mine], (tm_peer(i), f))

    @pl.when(is_owner)
    def _():
        pltpu.make_async_copy(gpart.at[mine], grecv.at[t], l_sem.at[0]).wait()

        def g_wait(i):
            n = tm_peer(i)
            remote(grecv.at[n], grecv.at[n], g_send.at[0], g_recv.at[n], (t, f)).wait_recv()

        each(1, TM, g_wait)
        total = grecv[0]
        for n in range(1, TM):
            total = total + grecv[n]
        total = total * (1.0 / TOTAL_ROWS)
        gm = jnp.concatenate([total[:, :64], total[:, 64:]], axis=0)
        perm[...] = jnp.zeros_like(perm)
        natural_rows(perm, gm)
        gm = perm[0:64, :].T
        natural_rows(perm, gm)
        eye = jnp.where(r == c, 1.0, 0.0).astype(jnp.float32)
        m = jnp.concatenate([perm[0:64, :], eye], axis=1)
        m = eliminate([m[8 * i : 8 * i + 8, :] for i in range(8)])
        for i in range(8):
            res[mine, 8 * i : 8 * i + 8, :] = m[i]
        each(1, TM, lambda i: r_copy(i).start())

    upper = c >= r

    def finish(k):
        @pl.when(jnp.logical_not(is_owner & (mine == k)))
        def _():
            remote(res.at[k], res.at[k], r_send.at[0], r_recv.at[k], (t, f)).wait_recv()

        v = res[k]
        factor_ref[k] = jnp.where(upper, v[:, :64], 0.0)[:COLS, :COLS]
        w = jnp.where(c <= r, v[:, 64:], 0.0)
        hi = w.astype(jnp.bfloat16)
        rest = w - hi.astype(jnp.float32)
        lo = rest.astype(jnp.bfloat16)
        low = (rest - lo.astype(jnp.float32)).astype(jnp.bfloat16)
        a = cols[k]
        out = jnp.dot(low, a, preferred_element_type=jnp.float32)
        out = out + jnp.dot(lo, a, preferred_element_type=jnp.float32)
        out = out + jnp.dot(hi, a, preferred_element_type=jnp.float32)
        basis_ref[k] = out[:COLS, :].astype(jnp.bfloat16)

    each(0, BINS, finish)

    for s in range(SUB):
        each(1, FREQ, lambda i: a_copy(i, s).wait_send())

    def b_wait(n):
        @pl.when(n != t)
        def _():
            b_copy(n).wait_send()

    each(0, TM, b_wait)
    for g in range(GROUPS):
        each(1, FREQ, lambda i: c_copy(i, g).wait_send())

    def g_wait_send(k):
        @pl.when(owner(k) != t)
        def _():
            g_copy(k).wait_send()

    each(0, BINS, g_wait_send)

    @pl.when(is_owner)
    def _():
        each(1, TM, lambda i: r_copy(i).wait_send())


def on_device(snapshots):
    band = jnp.asarray(band_table())
    bf16, f32 = jnp.bfloat16, jnp.float32
    dma = pltpu.SemaphoreType.DMA
    anywhere = pl.BlockSpec(memory_space=pl.ANY)
    vmem = pl.BlockSpec(memory_space=pltpu.VMEM)
    return pl.pallas_call(
        kernel,
        out_shape=(
            jax.ShapeDtypeStruct((BINS, COLS, ROWS_HERE), bf16),
            jax.ShapeDtypeStruct((BINS, COLS, COLS), f32),
        ),
        in_specs=[anywhere, anywhere],
        out_specs=(vmem, vmem),
        scratch_shapes=[
            pltpu.VMEM((K * TILE, DEPTH), bf16),
            pltpu.VMEM((TM, HALF, LANES), bf16),
            pltpu.VMEM((TM + 1, HALF, LANES), bf16),
            pltpu.VMEM((GROUPS, K * TILE, LANES), bf16),
            pltpu.VMEM((GROUPS, PART, ROWS_HERE), bf16),
            pltpu.VMEM((BINS, 64, ROWS_HERE), bf16),
            pltpu.VMEM((BINS, 32, 128), f32),
            pltpu.VMEM((TM, 32, 128), f32),
            pltpu.VMEM((BINS, 64, 128), f32),
            pltpu.VMEM((72, 64), f32),
            dma,
            dma((GROUPS,)),
            dma((FREQ, SUB)),
            dma((FREQ, SUB)),
            dma((TM,)),
            dma((TM,)),
            dma((FREQ, GROUPS)),
            dma((FREQ, GROUPS)),
            dma((BINS,)),
            dma((TM,)),
            dma((TM,)),
            dma((BINS,)),
        ],
        name="block_spectra_qr",
        compiler_params=pltpu.CompilerParams(
            collective_id=0, has_side_effects=True, vmem_limit_bytes=40 * 2**20
        ),
    )(snapshots, band)


def solution(mesh):
    return jax.shard_map(
        on_device,
        mesh=mesh,
        in_specs=(P("tm", "freq"),),
        out_specs=(P("freq", None, "tm"), P("freq", None, None)),
        check_vma=False,
    )
```

time: 602 us -> 109 us (0.18)
  waiting for transfers between devices: 185 us -> 0 us
  other arithmetic: 160 us -> 0 us
  local copies, waits for them, and re-layouts: 139 us -> 5.53 us
  Pallas kernels: 0 us -> 102 us
  blocking collectives: 91.3 us -> 0 us
  between operations: 14.2 us -> 0.65 us
  matrix products: 7.79 us -> 0 us
    another operation x8 -> x0, other arithmetic: 158 us -> none  [the longest x4 85.4 us: on_device(): lower_factor = jnp.linalg.cholesky(gram_matrix)]
    psum x1 -> x0, waiting for transfers between devices: 141 us -> none  [on_device(): gram_matrix = lax.psum(local_gram, 'tm') / total_rows]
    pallas_call x0 -> x1, Pallas kernels: none -> 102 us  [on_device(): pl.pallas_call(kernel, out_shape=(jax.ShapeDtypeStruct((BINS, COLS, ROWS_...]
    all_to_all x2 -> x0, blocking collectives: 91.3 us -> none  [the longest x1 61 us: on_device(): lax.all_to_all(lax.all_to_all(shaped, 'freq', split_axis=0, concat_axis=3...]
    unnamed x10 -> x6, local copies, waits for them, and re-layouts: 92.7 us -> 5.53 us
    ppermute x1 -> x0, waiting for transfers between devices: 44 us -> none  [passed_along(): return lax.ppermute(value, axis, pairs)]
    all_to_all x1 -> x0, local copies, waits for them, and re-layouts: 27.6 us -> none  [on_device(): lax.all_to_all(shaped, 'freq', split_axis=0, concat_axis=3, tiled=True)]
    slice x1 -> x0, local copies, waits for them, and re-layouts: 13.7 us -> none  [on_device(): columns = arrived[:, :, :tm_size - 1, :].reshape(groups, width, row_count)]
  transfers between devices with their start and end apart: 2 -> 0, of which waited for: 2 -> 0; matrix products, arithmetic and copies ran while one was open for 0% -> 0% of each run, Pallas kernels for 0% -> 0%
where the time goes in v1:
time: 109 us; the launch traced here: 108 us
  Pallas kernels  102 us (94%)
  local copies, waits for them, and re-layouts  5.53 us (5%)
    pallas_call x1, Pallas kernels, on_device(): pl.pallas_call(kernel, out_shape=(jax.ShapeDtypeStruct((BINS, COLS, ROWS_...  102 us
    unnamed x6, local copies, waits for them, and re-layouts  5.53 us

profile of v1, /device:TPU:16, one launch (start us, length us, event | category | flops | bytes accessed | tf_op | source)
XLA Modules:
  0.0 107.7 jit_solution(13945856259627915411)
XLA Ops:
  0.6 0.0 copy-start
  0.6 2.2 %copy-done = bf16[1920,1152]{1,0:T(8,128)(2,1)S(1)} copy-done((bf16[1920,1152]{1,0:T(8,128)(2,1)S(1)}, bf16[1920,1152]{1,0:T(8,128)(2,1)}, u32[]{:S(2)}) %copy-start) | copy-done | bytes 4423704
  2.9 0.0 copy-start.1
  2.9 1.2 %copy-done.1 = bf16[128,4096]{1,0:T(8,128)(2,1)S(1)} copy-done((bf16[128,4096]{1,0:T(8,128)(2,1)S(1)}, bf16[128,4096]{1,0:T(8,128)(2,1)}, u32[]{:S(2)}) %copy-start.1) | copy-done | bytes 1048600
  4.1 101.5 %block_spectra_qr.1 = (bf16[15,62,1024]{2,1,0:T(8,128)(2,1)S(1)}, f32[15,62,62]{2,1,0:T(8,128)S(1)}) custom-call(bf16[128,4096]{1,0:T(8,128)(2,1)S(1)} %copy-done.1, bf16[1920,1152]{1,0:T(8,128)(2,1)S(1)} %copy-done), custom_call_target="tpu_custom_call" | custom-call | tf_op jit(solution)/shard_map/block_spectra_qr/pallas_call | solution.py:340
  105.6 1.3 %copy.6 = bf16[15,62,1024]{2,1,0:T(8,128)(2,1)} copy(bf16[15,62,1024]{2,1,0:T(8,128)(2,1)S(1)} %get-tuple-element.4) | data formatting | bytes 3809280
  106.9 0.8 copy.7
Async XLA Ops:
  0.6 2.3 %copy-start = (bf16[1920,1152]{1,0:T(8,128)(2,1)S(1)}, bf16[1920,1152]{1,0:T(8,128)(2,1)}, u32[]{:S(2)}) copy-start(bf16[1920,1152]{1,0:T(8,128)(2,1)} %constant.2.clone.band_hbm) | copy-start | bytes 13271044
  2.9 1.2 %copy-start.1 = (bf16[128,4096]{1,0:T(8,128)(2,1)S(1)}, bf16[128,4096]{1,0:T(8,128)(2,1)}, u32[]{:S(2)}) copy-start(bf16[128,4096]{1,0:T(8,128)(2,1)} %x_ref.1) | copy-start | bytes 3145732

commit v2 on v1

--- a/solution.py
+++ b/solution.py
@@ -25,6 +25,9 @@
 DEPTH = SLABS * HALF
 SUB = 4
 ROWS_HERE = FREQ * LANES
+B_ORDER = (2, 6, 0, 4, 1, 7, 3, 5)
+B_EARLY = 3
+B_FLIGHT = 8
 TOTAL_ROWS = TM * ROWS_HERE
 
 
@@ -85,7 +88,7 @@
     x_ref, band_hbm, basis_ref, factor_ref,
     band, mid, xt, spec, held, cols, gpart, grecv, res, perm,
     band_sem, l_sem, a_send, a_recv, b_send, b_recv, c_send, c_recv,
-    g_send, g_recv, r_send, r_recv,
+    g_send, g_recv, z_send, y_send, r_recv,
 ):
     t = lax.axis_index("tm")
     f = lax.axis_index("freq")
@@ -127,37 +130,65 @@
         return remote(colblock(FREQ * s + to), mid.at[SUB * f + s], a_send.at[i, s],
                       a_recv.at[f, s], (t, to))
 
+    def own_copy(s):
+        return pltpu.make_async_copy(colblock(FREQ * s + f), mid.at[SUB * f + s], l_sem.at[s])
+
+    away = lax.rem(f - z + FREQ, FREQ)
+    early = away % 2 == 0
+
+    def a_start():
+        for s in range(SUB):
+            each(1, FREQ, lambda i: a_copy(i, s).start())
+
+    pl.when(early)(a_start)
     for s in range(SUB):
-        each(1, FREQ, lambda i: a_copy(i, s).start())
-        pltpu.make_async_copy(colblock(FREQ * s + f), mid.at[SUB * f + s], l_sem.at[s]).start()
+        own_copy(s).start()
+    xt[TM] = jnp.zeros((HALF, LANES), jnp.bfloat16)
     for s in range(SUB):
-        pltpu.make_async_copy(colblock(FREQ * s + f), mid.at[SUB * f + s], l_sem.at[s]).wait()
-
-    xt[TM] = jnp.zeros((HALF, LANES), jnp.bfloat16)
+        own_copy(s).wait()
 
     def b_copy(n):
         return remote(mid.at[n], xt.at[t], b_send.at[n], b_recv.at[t], (n, f))
 
-    def b_step(i):
-        d = i // SUB
-        dz = jnp.where(d % 2 == 1, (d + 1) // 2, FREQ - d // 2)
+    def b_steps(dz):
         ff = lax.rem(z + dz, FREQ)
-        s = lax.rem(y + i, SUB)
-        n = SUB * ff + s
-
-        @pl.when(ff != f)
-        def _():
-            remote(mid.at[n], mid.at[n], a_send.at[0, 0], a_recv.at[ff, s], (t, f)).wait_recv()
-
-        @pl.when(n != t)
-        def _():
-            b_copy(n).start()
-
-        @pl.when(n == t)
-        def _():
-            pltpu.make_async_copy(mid.at[n], xt.at[t], l_sem.at[0]).start()
-
-    each(0, TM, b_step)
+
+        def b_step(i):
+            s = lax.rem(y + i, SUB)
+            n = SUB * ff + s
+
+            @pl.when(ff != f)
+            def _():
+                remote(mid.at[n], mid.at[n], a_send.at[0, 0], a_recv.at[ff, s], (t, f)).wait_recv()
+
+            @pl.when(n != t)
+            def _():
+                b_copy(n).start()
+
+            @pl.when(n == t)
+            def _():
+                pltpu.make_async_copy(mid.at[n], xt.at[t], l_sem.at[0]).start()
+
+        each(0, SUB, b_step)
+
+    def b_done(dz):
+        ff = lax.rem(z + dz, FREQ)
+
+        def b_wait(i):
+            n = SUB * ff + lax.rem(y + i, SUB)
+
+            @pl.when(n != t)
+            def _():
+                b_copy(n).wait_send()
+
+        each(0, SUB, b_wait)
+
+    for i, dz in enumerate(B_ORDER):
+        if i == B_EARLY:
+            pl.when(jnp.logical_not(early))(a_start)
+        if i >= B_FLIGHT:
+            b_done(B_ORDER[i - B_FLIGHT])
+        b_steps(dz)
     pltpu.make_async_copy(mid.at[t], xt.at[t], l_sem.at[0]).wait()
     load_band.wait()
 
@@ -198,7 +229,8 @@
             part(i)
             c_copy(i, g).start()
 
-        each(1, FREQ, send_part)
+        for i in range(1, FREQ):
+            send_part(i)
         part(0)
         pltpu.make_async_copy(spec.at[g, piece(f), :], held.at[g, :, lanes_of(f)], l_sem.at[g]).start()
         return carry
@@ -222,16 +254,17 @@
 
     def bin_columns(k):
         return jnp.concatenate(
-            [held[g, pl.ds(pl.multiple_of(TILE * k, TILE), TILE), :] for g in range(GROUPS)], axis=0)
+            [held[g, pl.ds(TILE * k, TILE), :] for g in range(GROUPS)], axis=0)
 
     def g_copy(k):
         return remote(gpart.at[k], grecv.at[t], g_send.at[k], g_recv.at[t], (owner(k), f))
 
-    def gram(k):
+    for k in range(BINS):
         a = bin_columns(k)
         gm = nt_dot(a, a)
         gpart[k] = jnp.concatenate([gm[:32], gm[32:]], axis=1)
 
+    def g_start(k):
         @pl.when(owner(k) != t)
         def _():
             g_copy(k).start()
@@ -240,7 +273,7 @@
         def _():
             pltpu.make_async_copy(gpart.at[k], grecv.at[t], l_sem.at[0]).start()
 
-    each(0, BINS, gram)
+    each(0, BINS, g_start)
 
     r = lax.broadcasted_iota(jnp.int32, (64, 64), 0)
     c = lax.broadcasted_iota(jnp.int32, (64, 64), 1)
@@ -248,17 +281,24 @@
     to_row = BLOCKS * (c % TILE // GROUP) + block
     order = jnp.where((r == to_row) & (block < BLOCKS), 1.0, 0.0).astype(jnp.bfloat16)
 
-    def reorder(k):
+    for k in range(BINS):
         cols[k] = jnp.dot(order, bin_columns(k), preferred_element_type=jnp.float32).astype(
             jnp.bfloat16)
 
-    each(0, BINS, reorder)
-
     mine = t // 2
-    is_owner = (t % 2 == f % 2) & (mine < BINS)
-
-    def r_copy(i):
-        return remote(res.at[mine], res.at[mine], r_send.at[i], r_recv.at[mine], (tm_peer(i), f))
+    in_column = t % 2 == f % 2
+    is_owner = in_column & (mine < BINS)
+
+    def z_copy(i):
+        to = SUB * lax.rem(z + i, FREQ) + y
+        return remote(res.at[mine], res.at[mine], z_send.at[i], r_recv.at[mine], (to, f))
+
+    def y_copy(k, i):
+        to = SUB * z + lax.rem(y + i, SUB)
+        return remote(res.at[k], res.at[k], y_send.at[k // 2, i], r_recv.at[k], (to, f))
+
+    def received(k):
+        remote(res.at[k], res.at[k], z_send.at[0], r_recv.at[k], (t, f)).wait_recv()
 
     @pl.when(is_owner)
     def _():
@@ -281,20 +321,37 @@
         eye = jnp.where(r == c, 1.0, 0.0).astype(jnp.float32)
         m = jnp.concatenate([perm[0:64, :], eye], axis=1)
         m = eliminate([m[8 * i : 8 * i + 8, :] for i in range(8)])
-        for i in range(8):
-            res[mine, 8 * i : 8 * i + 8, :] = m[i]
-        each(1, TM, lambda i: r_copy(i).start())
-
-    upper = c >= r
-
-    def finish(k):
-        @pl.when(jnp.logical_not(is_owner & (mine == k)))
-        def _():
-            remote(res.at[k], res.at[k], r_send.at[0], r_recv.at[k], (t, f)).wait_recv()
-
+        m = jnp.concatenate(m, axis=0)
+        both = jnp.where(c >= r, m[:, :64], m[:, 64:])
+        res[mine] = jnp.concatenate([both[:32], both[32:]], axis=1)
+        each(1, FREQ, lambda i: z_copy(i).start())
+
+    def relay(i):
+        k = (SUB * lax.rem(z + i, FREQ) + y) // 2
+
+        @pl.when(k < BINS)
+        def _():
+            @pl.when(i > 0)
+            def _():
+                received(k)
+
+            each(1, SUB, lambda j: y_copy(k, j).start())
+
+    @pl.when(in_column)
+    def _():
+        each(0, FREQ, relay)
+
+    def arrived(k):
+        @pl.when(jnp.logical_not(in_column & ((2 * k + f % 2) % SUB == y)))
+        def _():
+            received(k)
+
+    each(0, BINS, arrived)
+    for k in range(BINS):
         v = res[k]
-        factor_ref[k] = jnp.where(upper, v[:, :64], 0.0)[:COLS, :COLS]
-        w = jnp.where(c <= r, v[:, 64:], 0.0)
+        both = jnp.concatenate([v[:, :64], v[:, 64:]], axis=0)
+        factor_ref[k] = jnp.where(c >= r, both, 0.0)[:COLS, :COLS]
+        w = jnp.where(c < r, both, jnp.where(c == r, 1.0 / both, 0.0))
         hi = w.astype(jnp.bfloat16)
         rest = w - hi.astype(jnp.float32)
         lo = rest.astype(jnp.bfloat16)
@@ -305,17 +362,11 @@
         out = out + jnp.dot(hi, a, preferred_element_type=jnp.float32)
         basis_ref[k] = out[:COLS, :].astype(jnp.bfloat16)
 
-    each(0, BINS, finish)
-
     for s in range(SUB):
         each(1, FREQ, lambda i: a_copy(i, s).wait_send())
 
-    def b_wait(n):
-        @pl.when(n != t)
-        def _():
-            b_copy(n).wait_send()
-
-    each(0, TM, b_wait)
+    for dz in B_ORDER[FREQ - B_FLIGHT :]:
+        b_done(dz)
     for g in range(GROUPS):
         each(1, FREQ, lambda i: c_copy(i, g).wait_send())
 
@@ -328,14 +379,25 @@
 
     @pl.when(is_owner)
     def _():
-        each(1, TM, lambda i: r_copy(i).wait_send())
+        each(1, FREQ, lambda i: z_copy(i).wait_send())
+
+    def relay_wait(i):
+        k = (SUB * lax.rem(z + i, FREQ) + y) // 2
+
+        @pl.when(k < BINS)
+        def _():
+            each(1, SUB, lambda j: y_copy(k, j).wait_send())
+
+    @pl.when(in_column)
+    def _():
+        each(0, FREQ, relay_wait)
 
 
 def on_device(snapshots):
     band = jnp.asarray(band_table())
     bf16, f32 = jnp.bfloat16, jnp.float32
     dma = pltpu.SemaphoreType.DMA
-    anywhere = pl.BlockSpec(memory_space=pl.ANY)
+    hbm = pl.BlockSpec(memory_space=pltpu.HBM)
     vmem = pl.BlockSpec(memory_space=pltpu.VMEM)
     return pl.pallas_call(
         kernel,
@@ -343,7 +405,7 @@
             jax.ShapeDtypeStruct((BINS, COLS, ROWS_HERE), bf16),
             jax.ShapeDtypeStruct((BINS, COLS, COLS), f32),
         ),
-        in_specs=[anywhere, anywhere],
+        in_specs=[hbm, hbm],
         out_specs=(vmem, vmem),
         scratch_shapes=[
             pltpu.VMEM((K * TILE, DEPTH), bf16),
@@ -354,7 +416,7 @@
             pltpu.VMEM((BINS, 64, ROWS_HERE), bf16),
             pltpu.VMEM((BINS, 32, 128), f32),
             pltpu.VMEM((TM, 32, 128), f32),
-            pltpu.VMEM((BINS, 64, 128), f32),
+            pltpu.VMEM((BINS, 32, 128), f32),
             pltpu.VMEM((72, 64), f32),
             dma,
             dma((GROUPS,)),
@@ -366,12 +428,13 @@
             dma((FREQ, GROUPS)),
             dma((BINS,)),
             dma((TM,)),
-            dma((TM,)),
+            dma((FREQ,)),
+            dma((FREQ, SUB)),
             dma((BINS,)),
         ],
         name="block_spectra_qr",
         compiler_params=pltpu.CompilerParams(
-            collective_id=0, has_side_effects=True, vmem_limit_bytes=40 * 2**20
+            collective_id=0, has_side_effects=True, vmem_limit_bytes=60 * 2**20
         ),
     )(snapshots, band)
 

time: 109 us -> 97.7 us (0.90)
  Pallas kernels: 102 us -> 92.4 us
  local copies, waits for them, and re-layouts: 5.53 us -> 3.87 us
    pallas_call x1, Pallas kernels: 102 us -> 92.4 us  [on_device(): pl.pallas_call(kernel, out_shape=(jax.ShapeDtypeStruct((BINS, COLS, ROWS_...]
    unnamed x6 -> x4, local copies, waits for them, and re-layouts: 5.53 us -> 3.87 us
where the time goes in v2:
time: 97.7 us; the launch traced here: 96.9 us
  Pallas kernels  92.4 us (95%)
  local copies, waits for them, and re-layouts  3.87 us (4%)
    pallas_call x1, Pallas kernels, on_device(): pl.pallas_call(kernel, out_shape=(jax.ShapeDtypeStruct((BINS, COLS, ROWS_...  92.4 us
    unnamed x4, local copies, waits for them, and re-layouts  3.87 us

profile of v2, /device:TPU:16, one launch (start us, length us, event | category | flops | bytes accessed | tf_op | source)
XLA Modules:
  0.0 96.9 jit_solution(13829655634931730586)
XLA Ops:
  0.6 92.4 %block_spectra_qr.1 = (bf16[15,62,1024]{2,1,0:T(8,128)(2,1)}, f32[15,62,62]{2,1,0:T(8,128)}) custom-call(bf16[128,4096]{1,0:T(8,128)(2,1)} %x_ref.1, bf16[1920,1152]{1,0:T(8,128)(2,1)} %constant.2.clone.band_hbm), custom_call_target="tpu_custom_call" | custom-call | tf_op jit(solution)/shard_map/block_spectra_qr/pallas_call | solution.py:402
  93.0 0.0 copy-start
  93.0 3.1 %copy.6 = bf16[15,62,1024]{2,1,0:T(8,128)(2,1)} copy(bf16[15,62,1024]{2,1,0:T(8,128)(2,1)} %get-tuple-element.4) | data formatting | bytes 3809280
  96.1 0.0 copy-done
  96.1 0.8 copy.7
Async XLA Ops:
  93.0 3.1 %copy-start = (f32[15,62,62]{2,1,0:T(8,128)S(1)}, f32[15,62,62]{2,1,0:T(8,128)}, u32[]{:S(2)}) copy-start(f32[15,62,62]{2,1,0:T(8,128)} %get-tuple-element.5) | copy-start | bytes 691924

commit v3 on v2

v3 whole, which is shorter than its diff:
```python
import math

import jax
import jax.numpy as jnp
import numpy as np
from jax import lax
from jax.experimental import pallas as pl
from jax.experimental.pallas import tpu as pltpu
from jax.sharding import PartitionSpec as P

MESH = pl.DeviceIdType.MESH
K = 120
HALF = 128
TM = 32
FREQ = 8
BINS = K // FREQ
BLOCKS = TM - 1
COLS = 2 * BLOCKS
GROUP = 8
GROUPS = TM // GROUP
TILE = 2 * GROUP
PART = BINS * TILE
LANES = 128
SLABS = GROUP + 1
DEPTH = SLABS * HALF
SUB = 4
ROWS_HERE = FREQ * LANES
LAST_BINS = 3
CHUNKS = BINS // LAST_BINS
SPREAD = 11
H_BIN = (0, 11, BINS)
H_ROW = tuple(TILE * k for k in H_BIN[:2])
H_ROWS = tuple(TILE * (hi - lo) for lo, hi in zip(H_BIN, H_BIN[1:]))
B_ORDER = (2, 6, 4, 0, 1, 7, 3, 5)
B_EARLY = 4
TOTAL_ROWS = TM * ROWS_HERE


def band_table():
    bins = np.arange(1, K + 1, dtype=np.int64)[:, None]
    sample = np.arange(2 * HALF, dtype=np.int64)[None, :]
    phase = (bins * sample % (2 * HALF)) * (2.0 * math.pi / (2 * HALF))
    window = 0.5 - 0.5 * np.cos(sample * (2.0 * math.pi / (2 * HALF)))
    table = np.stack([window * np.cos(phase), -window * np.sin(phase)], axis=1)
    table = table.astype(np.float32)
    band = np.zeros((K, 2, GROUP, SLABS * HALF), np.float32)
    for b in range(GROUP):
        band[:, :, b, b * HALF : (b + 2) * HALF] = table
    return band.reshape(K * TILE, DEPTH).astype(jnp.bfloat16)


def nt_dot(a, b):
    return lax.dot_general(a, b, (((1,), (1,)), ((), ())), preferred_element_type=jnp.float32)


def natural_rows(dst, value):
    for p in range(2):
        for g in range(GROUPS):
            r = TILE * g + GROUP * p
            dst[pl.ds(BLOCKS * p + GROUP * g, GROUP), :] = value[r : r + GROUP, :]


def eliminate(m):
    row = lax.broadcasted_iota(jnp.int32, (8, 128), 0)
    full = (8, 128)
    for j in range(0, COLS, 2):
        b, s = divmod(j, 8)
        r0 = jnp.broadcast_to(m[b][s : s + 1, :], full)
        r1 = jnp.broadcast_to(m[b][s + 1 : s + 2, :], full)
        a00 = jnp.broadcast_to(m[b][s : s + 1, j : j + 1], full)
        a01 = jnp.broadcast_to(m[b][s : s + 1, j + 1 : j + 2], full)
        a11 = jnp.broadcast_to(m[b][s + 1 : s + 2, j + 1 : j + 2], full)
        i0 = lax.rsqrt(a00)
        l10 = a01 * i0
        i1 = lax.rsqrt(a11 - l10 * l10)
        q0 = r0 * i0
        q1 = (r1 - l10 * q0) * i1
        for i in range(b, 8):
            c0 = jnp.broadcast_to(m[i][:, j : j + 1], full)
            c1 = jnp.broadcast_to(m[i][:, j + 1 : j + 2], full)
            m0 = c0 * i0
            m1 = (c1 - l10 * m0) * i1
            u = m[i] - m0 * q0 - m1 * q1
            if i == b:
                u = jnp.where(row > s + 1, u, m[i])
                u = jnp.where(row == s, q0, u)
                u = jnp.where(row == s + 1, q1, u)
            m[i] = u
    return m


def kernel(
    x_ref, band_hbm, cols, res,
    band, mid, xt, spec, held, gpart, grecv, perm,
    band_sem, l_sem, a_send, a_recv, b_send, b_recv, c_send, c_recv,
    g_send, g_recv, z_send, z_recv, y_send, y_recv,
):
    t = lax.axis_index("tm")
    f = lax.axis_index("freq")
    z, y = t // SUB, t % SUB

    def colblock(j):
        return x_ref.at[:, pl.ds(pl.multiple_of(j * LANES, LANES), LANES)]

    def freq_peer(i):
        return lax.rem(f + i, FREQ)

    def tm_peer(i):
        return lax.rem(t + i, TM)

    def remote(src, dst, send, recv, to):
        return pltpu.make_async_remote_copy(
            src, dst, send, recv, device_id=to, device_id_type=MESH
        )

    def each(lo, hi, body):
        def step(i, carry):
            body(i)
            return carry

        lax.fori_loop(lo, hi, step, 0)

    load_band = pltpu.make_async_copy(band_hbm, band, band_sem)
    load_band.start()

    barrier = pltpu.get_barrier_semaphore()
    each(1, FREQ, lambda i: pl.semaphore_signal(
        barrier, inc=1, device_id=(t, freq_peer(i)), device_id_type=MESH))
    each(1, TM, lambda i: pl.semaphore_signal(
        barrier, inc=1, device_id=(tm_peer(i), f), device_id_type=MESH))
    pl.semaphore_wait(barrier, FREQ - 1 + TM - 1)

    def a_copy(i, s):
        to = freq_peer(i)
        return remote(colblock(FREQ * s + to), mid.at[SUB * f + s], a_send, a_recv.at[f], (t, to))

    def own_copy(s):
        return pltpu.make_async_copy(colblock(FREQ * s + f), mid.at[SUB * f + s], l_sem.at[s])

    away = lax.rem(f - z + FREQ, FREQ)
    early = away % 2 == 0

    def a_start():
        def a_peer(i):
            for s in range(SUB):
                a_copy(i, s).start()

        each(1, FREQ, a_peer)

    pl.when(early)(a_start)
    for s in range(SUB):
        own_copy(s).start()
    xt[TM] = jnp.zeros((HALF, LANES), jnp.bfloat16)
    for s in range(SUB):
        own_copy(s).wait()

    def b_copy(n):
        return remote(mid.at[n], xt.at[t], b_send, b_recv.at[t], (n, f))

    def b_steps(dz):
        ff = lax.rem(z + dz, FREQ)

        @pl.when(ff != f)
        def _():
            part = mid.at[pl.ds(SUB * ff, SUB)]
            remote(part, part, a_send, a_recv.at[ff], (t, f)).wait_recv()

        for i in range(SUB):
            n = SUB * ff + lax.rem(y + i, SUB)
            if i > 0 or dz > 0:
                b_copy(n).start()
            else:
                pltpu.make_async_copy(mid.at[n], xt.at[t], l_sem.at[0]).start()

    for i, dz in enumerate(B_ORDER):
        if i == B_EARLY:
            pl.when(jnp.logical_not(early))(a_start)
        b_steps(dz)
    pltpu.make_async_copy(mid.at[t], xt.at[t], l_sem.at[0]).wait()
    load_band.wait()

    first = lax.rem(lax.rem(z + FREQ - 1, FREQ) // 2, GROUPS)

    def lanes_of(ff):
        return pl.ds(pl.multiple_of(ff * LANES, LANES), LANES)

    def piece(ff, h):
        return pl.ds(pl.multiple_of(ff * PART + H_ROW[h], TILE), H_ROWS[h])

    def c_copy(i, g, h):
        to = freq_peer(i)
        return remote(spec.at[g, piece(to, h), :],
                      held.at[g, pl.ds(H_ROW[h], H_ROWS[h]), lanes_of(f)],
                      c_send.at[g, h], c_recv.at[g, h], (t, to))

    def wait_slab(i):
        n = lax.rem(GROUP * first + i, TM)

        @pl.when(n != t)
        def _():
            remote(xt.at[n], xt.at[n], b_send, b_recv.at[n], (t, f)).wait_recv()

    def make_group(g, h):
        stack = xt[pl.ds(GROUP * g, SLABS)].reshape(DEPTH, LANES)

        def part(i):
            value = jnp.dot(band[piece(freq_peer(i), h), :], stack, preferred_element_type=jnp.float32)
            return value.astype(jnp.bfloat16)

        for i in range(1, FREQ):
            spec[g, piece(freq_peer(i), h), :] = part(i)
            c_copy(i, g, h).start()
        held[g, pl.ds(H_ROW[h], H_ROWS[h]), lanes_of(f)] = part(0)

    def first_half(step):
        lo = jnp.where(step == 0, 0, GROUP * step + 1)
        hi = jnp.minimum(GROUP * step + GROUP + 1, TM)
        each(lo, hi, wait_slab)
        make_group(lax.rem(first + step, GROUPS), 0)

    each(0, GROUPS, first_half)
    each(0, GROUPS, lambda step: make_group(lax.rem(first + step, GROUPS), 1))

    def others(g, h):
        part = held.at[g, pl.ds(H_ROW[h], H_ROWS[h]), pl.ds(0, (FREQ - 1) * LANES)]
        return remote(part, part, c_send.at[g, h], c_recv.at[g, h], (t, f))

    part = mid.at[pl.ds(0, SUB * (FREQ - 1))]
    remote(part, part, a_send, b_send, (t, f)).wait_send()
    part = mid.at[pl.ds(0, TM - 1)]
    remote(part, part, b_send, a_send, (t, f)).wait_send()

    def owner(k):
        return 2 * lax.rem(SPREAD * k, BINS) + f % 2

    def bin_columns(k):
        return jnp.concatenate(
            [held[g, pl.ds(TILE * k, TILE), :] for g in range(GROUPS)], axis=0)

    def g_copy(k):
        return remote(gpart.at[k], grecv.at[t], g_send, g_recv, (owner(k), f))

    def g_start(k):
        @pl.when(owner(k) != t)
        def _():
            g_copy(k).start()

        @pl.when(owner(k) == t)
        def _():
            pltpu.make_async_copy(gpart.at[k], grecv.at[t], l_sem.at[0]).start()

    r = lax.broadcasted_iota(jnp.int32, (64, 64), 0)
    c = lax.broadcasted_iota(jnp.int32, (64, 64), 1)
    block = GROUP * (c // TILE) + c % GROUP
    to_row = BLOCKS * (c % TILE // GROUP) + block
    order = jnp.where((r == to_row) & (block < BLOCKS), 1.0, 0.0).astype(jnp.bfloat16)

    for h in range(2):
        bins = range(H_BIN[h], H_BIN[h + 1])
        each(0, GROUPS, lambda g: others(g, h).wait_recv())
        for k in bins:
            a = bin_columns(k)
            gm = nt_dot(a, a)
            gpart[k] = jnp.concatenate([gm[:32], gm[32:]], axis=1)
        each(bins.start, bins.stop, g_start)
        for k in bins:
            cols[k] = jnp.dot(order, bin_columns(k), preferred_element_type=jnp.float32).astype(
                jnp.bfloat16)

    in_column = t % 2 == f % 2

    def column_bin(zz):
        return lax.rem(SPREAD * ((SUB * zz + y) // 2), BINS)

    def column_has(zz):
        return (SUB * zz + y) // 2 < BINS

    mine = column_bin(z)
    is_owner = in_column & column_has(z)

    def z_copy(i):
        to = SUB * lax.rem(z + i, FREQ) + y
        return remote(res.at[mine], res.at[mine], z_send, z_recv.at[z], (to, f))

    def y_copy(zz, i):
        k = column_bin(zz)
        to = SUB * z + lax.rem(y + i, SUB)
        return remote(res.at[k], res.at[k], y_send, y_recv, (to, f))

    def sized(n, send, recv):
        return remote(grecv.at[pl.ds(0, n)], grecv.at[pl.ds(0, n)], send, recv, (t, f))

    def sends_over(n):
        for h in range(2):
            each(0, GROUPS, lambda g: others(g, h).wait_send())
        sized(n, g_send, y_send).wait_send()

    @pl.when(jnp.logical_not(is_owner))
    def _():
        sends_over(BINS)

    @pl.when(is_owner)
    def _():
        pltpu.make_async_copy(gpart.at[mine], grecv.at[t], l_sem.at[0]).wait()

        sized(TM - 1, y_send, g_recv).wait_recv()
        total = grecv[0]
        for n in range(1, TM):
            total = total + grecv[n]
        total = total * (1.0 / TOTAL_ROWS)
        gm = jnp.concatenate([total[:, :64], total[:, 64:]], axis=0)
        perm[...] = jnp.zeros_like(perm)
        natural_rows(perm, gm)
        gm = perm[0:64, :].T
        natural_rows(perm, gm)
        eye = jnp.where(r == c, 1.0, 0.0).astype(jnp.float32)
        m = jnp.concatenate([perm[0:64, :], eye], axis=1)
        m = eliminate([m[8 * i : 8 * i + 8, :] for i in range(8)])
        m = jnp.concatenate(m, axis=0)
        both = jnp.where(c >= r, m[:, :64], m[:, 64:])
        res[mine] = jnp.concatenate([both[:32], both[32:]], axis=1)
        each(1, FREQ, lambda i: z_copy(i).start())

    def relay(h):
        def step(i):
            zz = lax.rem(z + i, FREQ)
            k = column_bin(zz)

            @pl.when(column_has(zz) & (k >= H_BIN[h]) & (k < H_BIN[h + 1]))
            def _():
                @pl.when(i > 0)
                def _():
                    remote(res.at[k], res.at[k], z_send, z_recv.at[zz], (t, f)).wait_recv()

                for j in range(1, SUB):
                    y_copy(zz, j).start()

        each(0, FREQ, step)

    @pl.when(in_column)
    def _():
        relay(0)
        relay(1)

    @pl.when(is_owner)
    def _():
        sends_over(BINS - 1)
        sized(FREQ - 1, z_send, y_recv).wait_send()

    here = jnp.where(in_column, y // 2, 2)
    held_bins = (FREQ, FREQ - 1)
    for column in range(2):

        @pl.when(here == column)
        def _():
            sized(held_bins[1 - column], z_send, y_recv).wait_recv()
            sized((SUB - 1) * held_bins[column], y_send, y_recv).wait_send()

    @pl.when(here == 2)
    def _():
        sized(BINS, z_send, y_recv).wait_recv()


def last_kernel(cols_hbm, res_hbm, basis_hbm, factor_hbm, cols, res, basis, factor, in_sem, out_sem):
    def chunk(i):
        return pl.ds(LAST_BINS * i, LAST_BINS)

    loads = [pltpu.make_async_copy(res_hbm, res, in_sem.at[CHUNKS])]
    loads += [
        pltpu.make_async_copy(cols_hbm.at[chunk(i)], cols.at[chunk(i)], in_sem.at[i])
        for i in range(CHUNKS)
    ]
    stores = [
        pltpu.make_async_copy(basis.at[chunk(i)], basis_hbm.at[chunk(i)], out_sem.at[i])
        for i in range(CHUNKS)
    ]
    stores.append(pltpu.make_async_copy(factor, factor_hbm, out_sem.at[CHUNKS]))
    for load in loads:
        load.start()
    r = lax.broadcasted_iota(jnp.int32, (64, 64), 0)
    c = lax.broadcasted_iota(jnp.int32, (64, 64), 1)
    loads[0].wait()
    wide = []
    for k in range(BINS):
        v = res[k]
        both = jnp.concatenate([v[:, :64], v[:, 64:]], axis=0)
        factor[k] = jnp.where(c >= r, both, 0.0)[:COLS, :COLS]
        wide.append(jnp.where(c < r, both, jnp.where(c == r, 1.0 / both, 0.0)))
    stores[-1].start()
    for i in range(CHUNKS):
        loads[1 + i].wait()
        for k in range(LAST_BINS * i, LAST_BINS * (i + 1)):
            w = wide[k]
            hi = w.astype(jnp.bfloat16)
            rest = w - hi.astype(jnp.float32)
            lo = rest.astype(jnp.bfloat16)
            low = (rest - lo.astype(jnp.float32)).astype(jnp.bfloat16)
            a = cols[k]
            out = jnp.dot(low, a, preferred_element_type=jnp.float32)
            out = out + jnp.dot(lo, a, preferred_element_type=jnp.float32)
            out = out + jnp.dot(hi, a, preferred_element_type=jnp.float32)
            basis[k] = out[:COLS, :].astype(jnp.bfloat16)
        stores[i].start()
    for store in stores:
        store.wait()


def on_device(snapshots):
    band = jnp.asarray(band_table())
    bf16, f32 = jnp.bfloat16, jnp.float32
    dma = pltpu.SemaphoreType.DMA
    hbm = pl.BlockSpec(memory_space=pltpu.HBM)
    vmem = pl.BlockSpec(memory_space=pltpu.VMEM)
    cols, res = pl.pallas_call(
        kernel,
        out_shape=(
            jax.ShapeDtypeStruct((BINS, 64, ROWS_HERE), bf16),
            jax.ShapeDtypeStruct((BINS, 32, 128), f32),
        ),
        in_specs=[hbm, hbm],
        out_specs=(vmem, vmem),
        scratch_shapes=[
            pltpu.VMEM((K * TILE, DEPTH), bf16),
            pltpu.VMEM((TM, HALF, LANES), bf16),
            pltpu.VMEM((TM + 1, HALF, LANES), bf16),
            pltpu.VMEM((GROUPS, K * TILE, LANES), bf16),
            pltpu.VMEM((GROUPS, PART, ROWS_HERE), bf16),
            pltpu.VMEM((BINS, 32, 128), f32),
            pltpu.VMEM((TM, 32, 128), f32),
            pltpu.VMEM((72, 64), f32),
            dma,
            dma((GROUPS,)),
            dma,
            dma((FREQ,)),
            dma,
            dma((TM,)),
            dma((GROUPS, 2)),
            dma((GROUPS, 2)),
            dma,
            dma,
            dma,
            dma((FREQ,)),
            dma,
            dma,
        ],
        name="block_spectra_qr",
        compiler_params=pltpu.CompilerParams(
            collective_id=0, has_side_effects=True, vmem_limit_bytes=60 * 2**20
        ),
    )(snapshots, band)

    return pl.pallas_call(
        last_kernel,
        out_shape=(
            jax.ShapeDtypeStruct((BINS, COLS, ROWS_HERE), bf16),
            jax.ShapeDtypeStruct((BINS, COLS, COLS), f32),
        ),
        in_specs=[hbm, hbm],
        out_specs=(hbm, hbm),
        scratch_shapes=[
            pltpu.VMEM((BINS, 64, ROWS_HERE), bf16),
            pltpu.VMEM((BINS, 32, 128), f32),
            pltpu.VMEM((BINS, COLS, ROWS_HERE), bf16),
            pltpu.VMEM((BINS, COLS, COLS), f32),
            dma((CHUNKS + 1,)),
            dma((CHUNKS + 1,)),
        ],
        name="basis",
        compiler_params=pltpu.CompilerParams(vmem_limit_bytes=60 * 2**20),
    )(cols, res)


def solution(mesh):
    return jax.shard_map(
        on_device,
        mesh=mesh,
        in_specs=(P("tm", "freq"),),
        out_specs=(P("freq", None, "tm"), P("freq", None, None)),
        check_vma=False,
    )
```

time: 97.7 us -> 89.7 us (0.918)
  local copies, waits for them, and re-layouts: 3.87 us -> 0 us
  Pallas kernels: 92.4 us -> 88.9 us
    unnamed x4 -> x0, local copies, waits for them, and re-layouts: 3.87 us -> none
    pallas_call x1 -> x2, Pallas kernels: 92.4 us -> 88.9 us  [the longest x1 84.7 us: on_device(): pl.pallas_call(kernel, out_shape=(jax.ShapeDtypeStruct((BINS, 64, ROWS_HE...]
where the time goes in v3:
time: 89.7 us; the launch traced here: 89.5 us
  Pallas kernels  88.9 us (99%)
    pallas_call x1, Pallas kernels, on_device(): pl.pallas_call(kernel, out_shape=(jax.ShapeDtypeStruct((BINS, 64, ROWS_HE...  84.7 us
    pallas_call x1, Pallas kernels, on_device(): pl.pallas_call(last_kernel, out_shape=(jax.ShapeDtypeStruct((BINS, COLS,...  4.22 us

profile of v3, /device:TPU:16, one launch (start us, length us, event | category | flops | bytes accessed | tf_op | source)
XLA Modules:
  0.0 89.5 jit_solution(6554648870703855077)
XLA Ops:
  0.6 84.7 %block_spectra_qr.1 = (bf16[15,64,1024]{2,1,0:T(8,128)(2,1)}, f32[15,32,128]{2,1,0:T(8,128)}) custom-call(bf16[128,4096]{1,0:T(8,128)(2,1)} %x_ref.1, bf16[1920,1152]{1,0:T(8,128)(2,1)} %constant.2.clone.band_hbm), custom_call_target="tpu_custom_call" | custom-call | tf_op jit(solution)/shard_map/block_spectra_qr/pallas_call | solution.py:414
  85.3 4.2 %basis.1 = (bf16[15,62,1024]{2,1,0:T(8,128)(2,1)}, f32[15,62,62]{2,1,0:T(8,128)}) custom-call(bf16[15,64,1024]{2,1,0:T(8,128)(2,1)} %get-tuple-element.4.cols_hbm, f32[15,32,128]{2,1,0:T(8,128)} %get-tuple-element.5.res_hbm), custom_call_target="tpu_custom_call" | custom-call | tf_op jit(solution)/shard_map/basis/pallas_call | solution.py:452

commit v4 on v3

--- a/solution.py
+++ b/solution.py
@@ -62,37 +62,45 @@
 
 def eliminate(m):
     row = lax.broadcasted_iota(jnp.int32, (8, 128), 0)
-    full = (8, 128)
-    for j in range(0, COLS, 2):
-        b, s = divmod(j, 8)
-        r0 = jnp.broadcast_to(m[b][s : s + 1, :], full)
-        r1 = jnp.broadcast_to(m[b][s + 1 : s + 2, :], full)
-        a00 = jnp.broadcast_to(m[b][s : s + 1, j : j + 1], full)
-        a01 = jnp.broadcast_to(m[b][s : s + 1, j + 1 : j + 2], full)
-        a11 = jnp.broadcast_to(m[b][s + 1 : s + 2, j + 1 : j + 2], full)
-        i0 = lax.rsqrt(a00)
-        l10 = a01 * i0
-        i1 = lax.rsqrt(a11 - l10 * l10)
-        q0 = r0 * i0
-        q1 = (r1 - l10 * q0) * i1
-        for i in range(b, 8):
-            c0 = jnp.broadcast_to(m[i][:, j : j + 1], full)
-            c1 = jnp.broadcast_to(m[i][:, j + 1 : j + 2], full)
-            m0 = c0 * i0
-            m1 = (c1 - l10 * m0) * i1
-            u = m[i] - m0 * q0 - m1 * q1
-            if i == b:
-                u = jnp.where(row > s + 1, u, m[i])
-                u = jnp.where(row == s, q0, u)
-                u = jnp.where(row == s + 1, q1, u)
-            m[i] = u
+
+    def spread(v):
+        return jnp.broadcast_to(v, (8, 128))
+
+    for b in range(8):
+        j = 8 * b
+        width = min(8, COLS - j)
+        low = [[spread(m[b][q : q + 1, j + p : j + p + 1]) for p in range(q + 1)] for q in range(width)]
+        inv, done = [], []
+        for q in range(width):
+            for p in range(q):
+                low[q][q] = low[q][q] - low[q][p] * low[q][p]
+            inv.append(lax.rsqrt(low[q][q]))
+            for u in range(q + 1, width):
+                for p in range(q):
+                    low[u][q] = low[u][q] - low[u][p] * low[q][p]
+                low[u][q] = low[u][q] * inv[q]
+            v = spread(m[b][q : q + 1, :])
+            for p in range(q):
+                v = v - low[q][p] * done[p]
+            done.append(v * inv[q])
+        for i in range(b + 1, 8):
+            below = []
+            for q in range(width):
+                v = spread(m[i][:, j + q : j + q + 1])
+                for p in range(q):
+                    v = v - low[q][p] * below[p]
+                below.append(v * inv[q])
+            for q in range(width):
+                m[i] = m[i] - below[q] * done[q]
+        for q in range(width):
+            m[b] = jnp.where(row == q, done[q], m[b])
     return m
 
 
 def kernel(
-    x_ref, band_hbm, cols, res,
-    band, mid, xt, spec, held, gpart, grecv, perm,
-    band_sem, l_sem, a_send, a_recv, b_send, b_recv, c_send, c_recv,
+    x_ref, band_hbm, cols_hbm, res,
+    band, mid, xt, spec, held, cols, gpart, grecv, perm,
+    cols_sem, band_sem, l_sem, a_send, a_recv, b_send, b_recv, c_send, c_recv,
     g_send, g_recv, z_send, z_recv, y_send, y_recv,
 ):
     t = lax.axis_index("tm")
@@ -254,6 +262,10 @@
     block = GROUP * (c // TILE) + c % GROUP
     to_row = BLOCKS * (c % TILE // GROUP) + block
     order = jnp.where((r == to_row) & (block < BLOCKS), 1.0, 0.0).astype(jnp.bfloat16)
+
+    def cols_out(h):
+        part = pl.ds(H_BIN[h], H_BIN[h + 1] - H_BIN[h])
+        return pltpu.make_async_copy(cols.at[part], cols_hbm.at[part], cols_sem.at[h])
 
     for h in range(2):
         bins = range(H_BIN[h], H_BIN[h + 1])
@@ -266,6 +278,7 @@
         for k in bins:
             cols[k] = jnp.dot(order, bin_columns(k), preferred_element_type=jnp.float32).astype(
                 jnp.bfloat16)
+        cols_out(h).start()
 
     in_column = t % 2 == f % 2
 
@@ -346,6 +359,9 @@
     def _():
         sends_over(BINS - 1)
         sized(FREQ - 1, z_send, y_recv).wait_send()
+
+    for h in range(2):
+        cols_out(h).wait()
 
     here = jnp.where(in_column, y // 2, 2)
     held_bins = (FREQ, FREQ - 1)
@@ -418,16 +434,18 @@
             jax.ShapeDtypeStruct((BINS, 32, 128), f32),
         ),
         in_specs=[hbm, hbm],
-        out_specs=(vmem, vmem),
+        out_specs=(hbm, vmem),
         scratch_shapes=[
             pltpu.VMEM((K * TILE, DEPTH), bf16),
             pltpu.VMEM((TM, HALF, LANES), bf16),
             pltpu.VMEM((TM + 1, HALF, LANES), bf16),
             pltpu.VMEM((GROUPS, K * TILE, LANES), bf16),
             pltpu.VMEM((GROUPS, PART, ROWS_HERE), bf16),
+            pltpu.VMEM((BINS, 64, ROWS_HERE), bf16),
             pltpu.VMEM((BINS, 32, 128), f32),
             pltpu.VMEM((TM, 32, 128), f32),
             pltpu.VMEM((72, 64), f32),
+            dma((2,)),
             dma,
             dma((GROUPS,)),
             dma,

time: 89.7 us -> 86.3 us (0.962)
  Pallas kernels: 88.9 us -> 85.4 us
    pallas_call x1, Pallas kernels: 84.7 us -> 81.2 us  [on_device(): pl.pallas_call(kernel, out_shape=(jax.ShapeDtypeStruct((BINS, 64, ROWS_HE...]
where the time goes in v4:
time: 86.3 us; the launch traced here: 86.1 us
  Pallas kernels  85.4 us (99%)
    pallas_call x1, Pallas kernels, on_device(): pl.pallas_call(kernel, out_shape=(jax.ShapeDtypeStruct((BINS, 64, ROWS_HE...  81.2 us
    pallas_call x1, Pallas kernels, on_device(): pl.pallas_call(last_kernel, out_shape=(jax.ShapeDtypeStruct((BINS, COLS,...  4.22 us

profile of v4, /device:TPU:16, one launch (start us, length us, event | category | flops | bytes accessed | tf_op | source)
XLA Modules:
  0.0 86.1 jit_solution(6926533130420756555)
XLA Ops:
  0.6 81.2 %block_spectra_qr.1 = (bf16[15,64,1024]{2,1,0:T(8,128)(2,1)}, f32[15,32,128]{2,1,0:T(8,128)}) custom-call(bf16[128,4096]{1,0:T(8,128)(2,1)} %x_ref.1, bf16[1920,1152]{1,0:T(8,128)(2,1)} %constant.2.clone.band_hbm), custom_call_target="tpu_custom_call" | custom-call | tf_op jit(solution)/shard_map/block_spectra_qr/pallas_call | solution.py:430
  81.9 4.2 %basis.1 = (bf16[15,62,1024]{2,1,0:T(8,128)(2,1)}, f32[15,62,62]{2,1,0:T(8,128)}) custom-call(bf16[15,64,1024]{2,1,0:T(8,128)(2,1)} %get-tuple-element.4.cols_hbm, f32[15,32,128]{2,1,0:T(8,128)} %get-tuple-element.5.res_hbm), custom_call_target="tpu_custom_call" | custom-call | tf_op jit(solution)/shard_map/basis/pallas_call | solution.py:470

commit v5 on v4

--- a/solution.py
+++ b/solution.py
@@ -31,8 +31,10 @@
 H_BIN = (0, 11, BINS)
 H_ROW = tuple(TILE * k for k in H_BIN[:2])
 H_ROWS = tuple(TILE * (hi - lo) for lo, hi in zip(H_BIN, H_BIN[1:]))
-B_ORDER = (2, 6, 4, 0, 1, 7, 3, 5)
-B_EARLY = 4
+Z_ORDER = (4, 3, 5, 2, 6, 1, 7)
+X_ORDER = (2, 6, 4, 3, 7, 5, 1)
+B_EARLY = ((2, 6, 4), (0,))
+B_LATE = ((1, 7), (3, 5))
 TOTAL_ROWS = TM * ROWS_HERE
 
 
@@ -132,10 +134,10 @@
     load_band.start()
 
     barrier = pltpu.get_barrier_semaphore()
-    each(1, FREQ, lambda i: pl.semaphore_signal(
-        barrier, inc=1, device_id=(t, freq_peer(i)), device_id_type=MESH))
-    each(1, TM, lambda i: pl.semaphore_signal(
-        barrier, inc=1, device_id=(tm_peer(i), f), device_id_type=MESH))
+    for i in range(1, FREQ):
+        pl.semaphore_signal(barrier, inc=1, device_id=(t, freq_peer(i)), device_id_type=MESH)
+    for i in range(1, TM):
+        pl.semaphore_signal(barrier, inc=1, device_id=(tm_peer(i), f), device_id_type=MESH)
     pl.semaphore_wait(barrier, FREQ - 1 + TM - 1)
 
     def a_copy(i, s):
@@ -153,7 +155,8 @@
             for s in range(SUB):
                 a_copy(i, s).start()
 
-        each(1, FREQ, a_peer)
+        for i in X_ORDER:
+            a_peer(i)
 
     pl.when(early)(a_start)
     for s in range(SUB):
@@ -165,25 +168,28 @@
     def b_copy(n):
         return remote(mid.at[n], xt.at[t], b_send, b_recv.at[t], (n, f))
 
-    def b_steps(dz):
-        ff = lax.rem(z + dz, FREQ)
-
-        @pl.when(ff != f)
-        def _():
-            part = mid.at[pl.ds(SUB * ff, SUB)]
-            remote(part, part, a_send, a_recv.at[ff], (t, f)).wait_recv()
+    def b_round(planes):
+        sources = [(dz, lax.rem(z + dz, FREQ)) for dz in planes]
+        for _, ff in sources:
+
+            @pl.when(ff != f)
+            def _():
+                part = mid.at[pl.ds(SUB * ff, SUB)]
+                remote(part, part, a_send, a_recv.at[ff], (t, f)).wait_recv()
 
         for i in range(SUB):
-            n = SUB * ff + lax.rem(y + i, SUB)
-            if i > 0 or dz > 0:
-                b_copy(n).start()
-            else:
-                pltpu.make_async_copy(mid.at[n], xt.at[t], l_sem.at[0]).start()
-
-    for i, dz in enumerate(B_ORDER):
-        if i == B_EARLY:
-            pl.when(jnp.logical_not(early))(a_start)
-        b_steps(dz)
+            for dz, ff in sources:
+                n = SUB * ff + lax.rem(y + i, SUB)
+                if i > 0 or dz > 0:
+                    b_copy(n).start()
+                else:
+                    pltpu.make_async_copy(mid.at[n], xt.at[t], l_sem.at[0]).start()
+
+    for planes in B_EARLY:
+        b_round(planes)
+    pl.when(jnp.logical_not(early))(a_start)
+    for planes in B_LATE:
+        b_round(planes)
     pltpu.make_async_copy(mid.at[t], xt.at[t], l_sem.at[0]).wait()
     load_band.wait()
 
@@ -215,7 +221,7 @@
             value = jnp.dot(band[piece(freq_peer(i), h), :], stack, preferred_element_type=jnp.float32)
             return value.astype(jnp.bfloat16)
 
-        for i in range(1, FREQ):
+        for i in X_ORDER:
             spec[g, piece(freq_peer(i), h), :] = part(i)
             c_copy(i, g, h).start()
         held[g, pl.ds(H_ROW[h], H_ROWS[h]), lanes_of(f)] = part(0)
@@ -274,7 +280,8 @@
             a = bin_columns(k)
             gm = nt_dot(a, a)
             gpart[k] = jnp.concatenate([gm[:32], gm[32:]], axis=1)
-        each(bins.start, bins.stop, g_start)
+        for i in range(len(bins)):
+            g_start(bins.start + lax.rem(t + i, len(bins)))
         for k in bins:
             cols[k] = jnp.dot(order, bin_columns(k), preferred_element_type=jnp.float32).astype(
                 jnp.bfloat16)
@@ -332,7 +339,8 @@
         m = jnp.concatenate(m, axis=0)
         both = jnp.where(c >= r, m[:, :64], m[:, 64:])
         res[mine] = jnp.concatenate([both[:32], both[32:]], axis=1)
-        each(1, FREQ, lambda i: z_copy(i).start())
+        for i in Z_ORDER:
+            z_copy(i).start()
 
     def relay(h):
         def step(i):
@@ -341,14 +349,14 @@
 
             @pl.when(column_has(zz) & (k >= H_BIN[h]) & (k < H_BIN[h + 1]))
             def _():
-                @pl.when(i > 0)
-                def _():
+                if i > 0:
                     remote(res.at[k], res.at[k], z_send, z_recv.at[zz], (t, f)).wait_recv()
 
                 for j in range(1, SUB):
                     y_copy(zz, j).start()
 
-        each(0, FREQ, step)
+        for i in (0, *reversed(Z_ORDER)):
+            step(i)
 
     @pl.when(in_column)
     def _():

time: 86.3 us -> 83.1 us (0.963)
  Pallas kernels: 85.4 us -> 82.3 us
    pallas_call x1, Pallas kernels: 81.2 us -> 78 us  [on_device(): pl.pallas_call(kernel, out_shape=(jax.ShapeDtypeStruct((BINS, 64, ROWS_HE...]
where the time goes in v5:
time: 83.1 us; the launch traced here: 82.9 us
  Pallas kernels  82.3 us (99%)
    pallas_call x1, Pallas kernels, on_device(): pl.pallas_call(kernel, out_shape=(jax.ShapeDtypeStruct((BINS, 64, ROWS_HE...  78 us
    pallas_call x1, Pallas kernels, on_device(): pl.pallas_call(last_kernel, out_shape=(jax.ShapeDtypeStruct((BINS, COLS,...  4.22 us

profile of v5, /device:TPU:16, one launch (start us, length us, event | category | flops | bytes accessed | tf_op | source)
XLA Modules:
  0.0 82.9 jit_solution(11883555700112400868)
XLA Ops:
  0.6 78.0 %block_spectra_qr.1 = (bf16[15,64,1024]{2,1,0:T(8,128)(2,1)}, f32[15,32,128]{2,1,0:T(8,128)}) custom-call(bf16[128,4096]{1,0:T(8,128)(2,1)} %x_ref.1, bf16[1920,1152]{1,0:T(8,128)(2,1)} %constant.2.clone.band_hbm), custom_call_target="tpu_custom_call" | custom-call | tf_op jit(solution)/shard_map/block_spectra_qr/pallas_call | solution.py:438
  78.7 4.2 %basis.1 = (bf16[15,62,1024]{2,1,0:T(8,128)(2,1)}, f32[15,62,62]{2,1,0:T(8,128)}) custom-call(bf16[15,64,1024]{2,1,0:T(8,128)(2,1)} %get-tuple-element.4.cols_hbm, f32[15,32,128]{2,1,0:T(8,128)} %get-tuple-element.5.res_hbm), custom_call_target="tpu_custom_call" | custom-call | tf_op jit(solution)/shard_map/basis/pallas_call | solution.py:478

commit v6 on v5

--- a/solution.py
+++ b/solution.py
@@ -25,8 +25,7 @@
 DEPTH = SLABS * HALF
 SUB = 4
 ROWS_HERE = FREQ * LANES
-LAST_BINS = 3
-CHUNKS = BINS // LAST_BINS
+LAST_BINS = 5
 SPREAD = 11
 H_BIN = (0, 11, BINS)
 H_ROW = tuple(TILE * k for k in H_BIN[:2])
@@ -385,48 +384,23 @@
         sized(BINS, z_send, y_recv).wait_recv()
 
 
-def last_kernel(cols_hbm, res_hbm, basis_hbm, factor_hbm, cols, res, basis, factor, in_sem, out_sem):
-    def chunk(i):
-        return pl.ds(LAST_BINS * i, LAST_BINS)
-
-    loads = [pltpu.make_async_copy(res_hbm, res, in_sem.at[CHUNKS])]
-    loads += [
-        pltpu.make_async_copy(cols_hbm.at[chunk(i)], cols.at[chunk(i)], in_sem.at[i])
-        for i in range(CHUNKS)
-    ]
-    stores = [
-        pltpu.make_async_copy(basis.at[chunk(i)], basis_hbm.at[chunk(i)], out_sem.at[i])
-        for i in range(CHUNKS)
-    ]
-    stores.append(pltpu.make_async_copy(factor, factor_hbm, out_sem.at[CHUNKS]))
-    for load in loads:
-        load.start()
+def last_kernel(cols, res, basis, factor):
     r = lax.broadcasted_iota(jnp.int32, (64, 64), 0)
     c = lax.broadcasted_iota(jnp.int32, (64, 64), 1)
-    loads[0].wait()
-    wide = []
-    for k in range(BINS):
+    for k in range(LAST_BINS):
         v = res[k]
         both = jnp.concatenate([v[:, :64], v[:, 64:]], axis=0)
         factor[k] = jnp.where(c >= r, both, 0.0)[:COLS, :COLS]
-        wide.append(jnp.where(c < r, both, jnp.where(c == r, 1.0 / both, 0.0)))
-    stores[-1].start()
-    for i in range(CHUNKS):
-        loads[1 + i].wait()
-        for k in range(LAST_BINS * i, LAST_BINS * (i + 1)):
-            w = wide[k]
-            hi = w.astype(jnp.bfloat16)
-            rest = w - hi.astype(jnp.float32)
-            lo = rest.astype(jnp.bfloat16)
-            low = (rest - lo.astype(jnp.float32)).astype(jnp.bfloat16)
-            a = cols[k]
-            out = jnp.dot(low, a, preferred_element_type=jnp.float32)
-            out = out + jnp.dot(lo, a, preferred_element_type=jnp.float32)
-            out = out + jnp.dot(hi, a, preferred_element_type=jnp.float32)
-            basis[k] = out[:COLS, :].astype(jnp.bfloat16)
-        stores[i].start()
-    for store in stores:
-        store.wait()
+        w = jnp.where(c < r, both, jnp.where(c == r, 1.0 / both, 0.0))
+        hi = w.astype(jnp.bfloat16)
+        rest = w - hi.astype(jnp.float32)
+        lo = rest.astype(jnp.bfloat16)
+        low = (rest - lo.astype(jnp.float32)).astype(jnp.bfloat16)
+        a = cols[k]
+        out = jnp.dot(low, a, preferred_element_type=jnp.float32)
+        out = out + jnp.dot(lo, a, preferred_element_type=jnp.float32)
+        out = out + jnp.dot(hi, a, preferred_element_type=jnp.float32)
+        basis[k] = out[:COLS, :].astype(jnp.bfloat16)
 
 
 def on_device(snapshots):
@@ -475,22 +449,18 @@
         ),
     )(snapshots, band)
 
+    def blocks(*shape):
+        return pl.BlockSpec((LAST_BINS, *shape), lambda i: (i, 0, 0))
+
     return pl.pallas_call(
         last_kernel,
+        grid=(BINS // LAST_BINS,),
         out_shape=(
             jax.ShapeDtypeStruct((BINS, COLS, ROWS_HERE), bf16),
             jax.ShapeDtypeStruct((BINS, COLS, COLS), f32),
         ),
-        in_specs=[hbm, hbm],
-        out_specs=(hbm, hbm),
-        scratch_shapes=[
-            pltpu.VMEM((BINS, 64, ROWS_HERE), bf16),
-            pltpu.VMEM((BINS, 32, 128), f32),
-            pltpu.VMEM((BINS, COLS, ROWS_HERE), bf16),
-            pltpu.VMEM((BINS, COLS, COLS), f32),
-            dma((CHUNKS + 1,)),
-            dma((CHUNKS + 1,)),
-        ],
+        in_specs=[blocks(64, ROWS_HERE), blocks(32, 128)],
+        out_specs=(blocks(COLS, ROWS_HERE), blocks(COLS, COLS)),
         name="basis",
         compiler_params=pltpu.CompilerParams(vmem_limit_bytes=60 * 2**20),
     )(cols, res)

time: 83.1 us -> 83.6 us (level)
  no operation moved by 1% of the time
where the time goes in v6:
time: 83.6 us; the launch traced here: 83.4 us
  Pallas kernels  82.8 us (99%)
    pallas_call x1, Pallas kernels, on_device(): pl.pallas_call(kernel, out_shape=(jax.ShapeDtypeStruct((BINS, 64, ROWS_HE...  78 us
    pallas_call x1, Pallas kernels, on_device(): pl.pallas_call(last_kernel, grid=(BINS // LAST_BINS,), out_shape=(jax.Sha...  4.71 us

profile of v6, /device:TPU:16, one launch (start us, length us, event | category | flops | bytes accessed | tf_op | source)
XLA Modules:
  0.0 83.4 jit_solution(12423965454621326672)
XLA Ops:
  0.6 78.0 %block_spectra_qr.1 = (bf16[15,64,1024]{2,1,0:T(8,128)(2,1)}, f32[15,32,128]{2,1,0:T(8,128)}) custom-call(bf16[128,4096]{1,0:T(8,128)(2,1)} %x_ref.1, bf16[1920,1152]{1,0:T(8,128)(2,1)} %constant.2.clone.band_hbm), custom_call_target="tpu_custom_call" | custom-call | tf_op jit(solution)/shard_map/block_spectra_qr/pallas_call | solution.py:412
  78.7 4.7 %basis.1 = (bf16[15,62,1024]{2,1,0:T(8,128)(2,1)}, f32[15,62,62]{2,1,0:T(8,128)}) custom-call(bf16[15,64,1024]{2,1,0:T(8,128)(2,1)} %get-tuple-element.4.cols, f32[15,32,128]{2,1,0:T(8,128)} %get-tuple-element.5.res), custom_call_target="tpu_custom_call" | custom-call | tf_op jit(solution)/shard_map/basis/pallas_call | solution.py:455

commit v7 on v6

--- a/solution.py
+++ b/solution.py
@@ -27,7 +27,7 @@
 ROWS_HERE = FREQ * LANES
 LAST_BINS = 5
 SPREAD = 11
-H_BIN = (0, 11, BINS)
+H_BIN = (0, 12, BINS)
 H_ROW = tuple(TILE * k for k in H_BIN[:2])
 H_ROWS = tuple(TILE * (hi - lo) for lo, hi in zip(H_BIN, H_BIN[1:]))
 Z_ORDER = (4, 3, 5, 2, 6, 1, 7)
@@ -351,7 +351,7 @@
                 if i > 0:
                     remote(res.at[k], res.at[k], z_send, z_recv.at[zz], (t, f)).wait_recv()
 
-                for j in range(1, SUB):
+                for j in (2, 1, 3):
                     y_copy(zz, j).start()
 
         for i in (0, *reversed(Z_ORDER)):

time: 83.6 us -> 84.3 us (level)
  no operation moved by 1% of the time
where the time goes in v7:
time: 84.3 us; the launch traced here: 83.8 us
  Pallas kernels  83.1 us (99%)
    pallas_call x1, Pallas kernels, on_device(): pl.pallas_call(kernel, out_shape=(jax.ShapeDtypeStruct((BINS, 64, ROWS_HE...  78.4 us
    pallas_call x1, Pallas kernels, on_device(): pl.pallas_call(last_kernel, grid=(BINS // LAST_BINS,), out_shape=(jax.Sha...  4.71 us

profile of v7, /device:TPU:16, one launch (start us, length us, event | category | flops | bytes accessed | tf_op | source)
XLA Modules:
  0.0 83.8 jit_solution(7666869505755429923)
XLA Ops:
  0.6 78.4 %block_spectra_qr.1 = (bf16[15,64,1024]{2,1,0:T(8,128)(2,1)}, f32[15,32,128]{2,1,0:T(8,128)}) custom-call(bf16[128,4096]{1,0:T(8,128)(2,1)} %x_ref.1, bf16[1920,1152]{1,0:T(8,128)(2,1)} %constant.2.clone.band_hbm), custom_call_target="tpu_custom_call" | custom-call | tf_op jit(solution)/shard_map/block_spectra_qr/pallas_call | solution.py:412
  79.1 4.7 %basis.1 = (bf16[15,62,1024]{2,1,0:T(8,128)(2,1)}, f32[15,62,62]{2,1,0:T(8,128)}) custom-call(bf16[15,64,1024]{2,1,0:T(8,128)(2,1)} %get-tuple-element.4.cols, f32[15,32,128]{2,1,0:T(8,128)} %get-tuple-element.5.res), custom_call_target="tpu_custom_call" | custom-call | tf_op jit(solution)/shard_map/basis/pallas_call | solution.py:455
